TPU v7x, 32 devices: a whole 2x2x4 slice. The times are simulated.
32 devices in a mesh: groups: 2 (over y), dom: 4 (over z), mp: 4 (over x, core).
Axes of the slice: x: 2, y: 2, z: 4, core: 2. Of those that a mesh axis runs over, the one named last changes fastest.
Arguments:
- grid_feat: bfloat16 [8192, 227], P(('groups', 'dom')), parts along dimension 0, may hold values from -6 to 6
- mesh_base: bfloat16 [8192, 512], P(('groups', 'dom'), 'mp'), parts along dimension 0, may hold values from -6 to 6
- w_embed: bfloat16 [227, 512], P(None, 'mp'), may hold values from -0.375 to 0.375
- w_edge: bfloat16 [512, 512], P(None, 'mp'), may hold values from -0.25 to 0.25
- w_agg: bfloat16 [512, 512], P(None, 'mp'), may hold values from -0.25 to 0.25
- w_msg: bfloat16 [2, 512, 512], P(None, None, 'mp'), may hold values from -0.25 to 0.25
- w_upd: bfloat16 [2, 512, 512], P(None, None, 'mp'), may hold values from -0.25 to 0.25
- w_dec: bfloat16 [512, 512], P(None, 'mp'), may hold values from -0.25 to 0.25
- w_gup: bfloat16 [512, 512], P(None, 'mp'), may hold values from -0.25 to 0.25
- w_out: bfloat16 [512, 227], P('mp'), may hold values from -0.25 to 0.25
- enc_src: int32 [4, 2048], P('dom'), may hold values from 0 to 1023
- enc_slot: int32 [4, 2048], P('dom'), may hold values from 0 to 1279, as said below
- enc_wt: float32 [4, 2048], P('dom'), may hold values from 0.3 to 3
- enc_row: int32 [4, 256], P('dom'), may hold values from 0 to 1023
- mesh_src: int32 [4, 8192], P('dom'), may hold values from 0 to 1087, as said below
- mesh_dst: int32 [4, 8192], P('dom'), may hold values from 0 to 1023
- mesh_wt: float32 [4, 8192], P('dom'), may hold values from 0.05 to 0.5
- halo_rows: int32 [4, 64], replicated, may hold values from 0 to 1023
- dec_src: int32 [4, 3072], P('dom'), may hold values from 0 to 1151, as said below
- dec_dst: int32 [4, 3072], P('dom'), may hold values from 0 to 1023
- dec_wt: float32 [4, 3072], P('dom'), may hold values from 0.1 to 1
- dec_rows: int32 [4, 128], replicated, may hold values from 0 to 1023
Outputs:
- forecast: float32 [8192, 227], P(('groups', 'dom', 'mp')), parts along dimension 0
There are 2 independent parts, one for each index of `groups`. A program takes and returns all parts, laid end to end along the dimension named above; an argument that names none is the same for every part. Nothing has to cross between parts.
Inputs may be any that keep to these rules, and one draw needn't show every extreme that they name: `enc_slot`: in every patch every local mesh row and every neighbour slot is the target of some edge. `mesh_src`: in every patch every local mesh row and every boundary slot sends along some edge. `dec_src`: in every patch every local mesh row and every decoding slot sends along some edge.
All inputs are finite; a program needn't handle non-finite values.
Results may differ from a plain program's by a relative error of at most 0.015.
Values may be sent and summed in bfloat16 or wider, within the bound.
A program may use at most 64 MiB of HBM per device.

v0:
```python
import functools

import jax
import jax.numpy as jnp
from jax import lax
from jax.experimental import pallas as pl
from jax.experimental.pallas import tpu as pltpu
from jax.sharding import PartitionSpec as P

MESH = pl.DeviceIdType.MESH
BF = jnp.bfloat16
F32 = jnp.float32
CHUNK = 512
TILE = 256


def silu(v):
    h = 0.5 * v
    return h + h * jnp.tanh(h)


def mm(a, b):
    return jnp.dot(a, b, preferred_element_type=F32)


def mm_nt(a, b):
    return lax.dot_general(a, b, (((1,), (1,)), ((), ())), preferred_element_type=F32)


def kernel(
    n_dom,
    grid_feat, mesh_base, w_embed, w_edge, w_agg, w_msg, w_upd, w_dec, w_gup, w_out,
    enc_src, enc_slot, enc_wt, enc_row, mesh_src, mesh_dst, mesh_wt, halo_rows,
    dec_src, dec_dst, dec_wt, dec_rows,
    out,
    emb_s, wq, wo, base_s, grid_lat, sent, a_enc, acc_enc, a_mesh, acc_mesh, a_dec, acc_dec,
    pick_h, pick_d, enc_out, enc_in, esum, lat, msg, halo_out, halo_in, dec_out, dec_in,
    sib_send, sib_recv, x_send, x_recv, f_send, f_recv, b_send, b_recv,
    e_send, e_recv, h_send, h_recv, d_send, d_recv, g_send, g_recv,
):
    gd = grid_feat.shape[0]
    md = mesh_base.shape[0]
    half = md // 2
    quarter = gd // 4
    lat_w = wq.shape[2]
    cin = grid_feat.shape[1]
    cap = enc_row.shape[1] // 4
    hb = halo_rows.shape[1] // 4
    db = dec_rows.shape[1] // 4
    layers = w_msg.shape[0]
    width = n_dom // 4
    offsets = (1, n_dom - 1, width, n_dom - width)
    g = lax.axis_index("groups")
    d = lax.axis_index("dom")
    i = lax.axis_index("mp")
    c = lax.rem(i, 2)
    sib = i + 1 - 2 * c
    xp = lax.rem(i + 2, 4)
    xs = lax.rem(sib + 2, 4)

    peers = [(g, d, sib), (g, d, xp), (g, d, xs)]
    for o in sorted(set(o % n_dom for o in offsets)):
        peers.append((g, lax.rem(d + o, n_dom), i))
    barrier = pltpu.get_barrier_semaphore()
    for peer in peers:
        pl.semaphore_signal(barrier, inc=1, device_id=peer, device_id_type=MESH)

    emb_s[i] = jnp.zeros(emb_s.shape[1:], BF)
    emb_s[i, 0:cin, :] = w_embed[...]
    wo[i] = jnp.zeros(wo.shape[1:], BF)
    wo[i, :, 0:cin] = w_out[...]
    sources = [w_edge, w_agg]
    for l in range(layers):
        sources += [w_msg.at[l], w_upd.at[l]]
    sources += [w_dec, w_gup]
    n_w = len(sources)
    for k in range(n_w):
        wq[k, i] = sources[k][...]
    base_s[i] = mesh_base[pl.ds(pl.multiple_of(c * half, half), half), :]

    EMB, OUT = n_w, n_w + 1

    def slot(k, q):
        if k == EMB:
            return emb_s.at[q]
        if k == OUT:
            return wo.at[q]
        return wq.at[k, q]

    def copy(src, dst, ss, rs, dev):
        return pltpu.make_async_remote_copy(
            src_ref=src, dst_ref=dst, send_sem=ss, recv_sem=rs, device_id=dev, device_id_type=MESH
        )

    def to_sib(k):
        return copy(slot(k, i), slot(k, i), sib_send.at[k], sib_recv.at[k], (g, d, sib))

    def to_x(k):
        return copy(slot(k, i), slot(k, i), x_send.at[k], x_recv.at[k], (g, d, xp))

    def fwd(k):
        return copy(slot(k, xp), slot(k, xp), f_send.at[k], f_recv.at[k], (g, d, sib))

    my_rows = pl.ds(pl.multiple_of(c * half, half), half)
    sib_rows = pl.ds(pl.multiple_of((1 - c) * half, half), half)
    base_copies = [
        copy(mesh_base.at[sib_rows, :], base_s.at[i], b_send.at[0], b_recv.at[0], (g, d, sib)),
        copy(mesh_base.at[my_rows, :], base_s.at[i], b_send.at[1], b_recv.at[1], (g, d, xp)),
        copy(mesh_base.at[sib_rows, :], base_s.at[i], b_send.at[2], b_recv.at[2], (g, d, xs)),
    ]

    pl.semaphore_wait(barrier, len(peers))

    def launch(ks):
        for k in ks:
            to_x(k).start()
            to_sib(k).start()

    def relay(ks):
        for k in ks:
            to_x(k).wait_recv()
            fwd(k).start()

    def ready(ks):
        for k in ks:
            to_sib(k).wait_recv()
            fwd(k).wait_recv()

    launch([EMB, 0])
    for b in base_copies:
        b.start()
    launch([1])

    def build(src_ref, dst_ref, wt_ref, target_of, rows, cols, acc, lo, hi):
        def body(t, _):
            e = pl.ds(pl.multiple_of(t * CHUNK, CHUNK), CHUNK)
            tgt = target_of(lax.broadcasted_iota(jnp.int32, (rows, CHUNK), 0))
            dt = jnp.where(tgt == dst_ref[:, e], 1.0, 0.0).astype(BF)
            row = lax.broadcasted_iota(jnp.int32, (cols, CHUNK), 0)
            st = jnp.where(row == src_ref[:, e], wt_ref[:, e], 0.0).astype(BF)
            acc[...] += mm_nt(dt, st)
            return 0

        lax.fori_loop(lo, hi, body, 0)

    def enc_target(m):
        return jnp.where(m < half, m + c * half, m + (md - half))

    acc_enc[...] = jnp.zeros(acc_enc.shape, F32)
    build(enc_src, enc_slot, enc_wt, enc_target, half + 4 * cap, gd, acc_enc, 0, enc_src.shape[1] // CHUNK)
    a_enc[...] = acc_enc[...].astype(BF)

    def weight(k):
        return jnp.concatenate([wq[k, q] for q in range(4)], axis=1)

    def tiles(n, body):
        def step(t, _):
            body(pl.ds(pl.multiple_of(t * TILE, TILE), TILE))
            return 0

        lax.fori_loop(0, n // TILE, step, 0)

    relay([EMB, 0])
    ready([EMB])
    launch([2, 3])

    def embed(r):
        w = jnp.concatenate([emb_s[q] for q in range(4)], axis=1)[0:cin]
        grid_lat[r, :] = silu(mm(grid_feat[r, :], w)).astype(BF)

    tiles(gd, embed)
    ready([0])

    def edge(r):
        sent[r, :] = silu(mm(grid_lat[r, :], weight(0))).astype(BF)

    tiles(gd, edge)

    slots = pl.ds(half, 4 * cap)
    enc_out[...] = mm(a_enc[slots, :], sent[...]).astype(BF)
    enc_copies, halo_copies, dec_copies = [], [], []
    for j in range(4):
        peer = (g, lax.rem(d + offsets[j], n_dom), i)
        own = pl.ds(j * cap, cap)
        enc_copies.append(copy(enc_out.at[own, :], enc_in.at[own, :], e_send.at[j], e_recv.at[j], peer))
        enc_copies[-1].start()

    def enc_local(r):
        esum[r, :] = mm(a_enc[r, :], sent[...])

    tiles(half, enc_local)
    relay([1])

    def pick(rows_ref, ref):
        n = ref.shape[0]
        row = rows_ref[pl.ds(d, 1), :].astype(F32)
        col = jnp.broadcast_to(row, (128, n)).T
        lane = lax.broadcasted_iota(jnp.int32, (n, 128), 1).astype(F32)
        for b in range(md // 128):
            ref[:, b * 128 : (b + 1) * 128] = jnp.where(col == lane + 128.0 * b, 1.0, 0.0).astype(BF)

    pick(halo_rows, pick_h)
    pick(dec_rows, pick_d)

    acc_mesh[...] = jnp.zeros(acc_mesh.shape, F32)
    acc_dec[...] = jnp.zeros(acc_dec.shape, F32)
    mesh_chunks = mesh_src.shape[1] // CHUNK
    dec_chunks = dec_src.shape[1] // CHUNK
    mesh_cols = acc_mesh.shape[1]

    def mesh_target(m):
        return m + c * half

    def dec_target(m):
        return m + i * quarter

    def build_mesh(lo, hi):
        build(mesh_src, mesh_dst, mesh_wt, mesh_target, half, mesh_cols, acc_mesh, lo, hi)

    def build_dec(lo, hi):
        build(dec_src, dec_dst, dec_wt, dec_target, quarter, acc_dec.shape[1], acc_dec, lo, hi)

    build_mesh(0, mesh_chunks // 2)
    relay([2, 3])
    launch([4, 5])
    build_mesh(mesh_chunks // 2, mesh_chunks)
    a_mesh[...] = acc_mesh[...].astype(BF)
    relay([4, 5])
    launch([6, 7, OUT])

    for cp in enc_copies:
        cp.wait_recv()
    ready([1])
    for b in base_copies:
        b.wait_recv()

    def agg(r):
        m = lax.broadcasted_iota(jnp.int32, (TILE, 4 * cap), 0) + (c * half + r.start)
        place = jnp.where(m == enc_row[...], 1.0, 0.0).astype(BF)
        total = (esum[r, :] + mm(place, enc_in[...])).astype(BF)
        base = jnp.concatenate([base_s[q, r, :] for q in range(4)], axis=1).astype(F32)
        lat[r, :] = (base + silu(mm(total, weight(1)))).astype(BF)

    tiles(half, agg)

    share_copies = []

    def share(k, t):
        def body(r):
            there = pl.ds(pl.multiple_of(c * half + r.start, TILE), TILE)
            msg[t, there, :] = silu(mm(lat[r, :], weight(k))).astype(BF)

        tiles(half, body)
        cp = copy(msg.at[t, my_rows, :], msg.at[t, my_rows, :], g_send.at[t], g_recv.at[t], (g, d, sib))
        cp.start()
        share_copies.append(cp)
        return cp

    for l in range(layers):
        kw = 2 + 2 * l
        ready([kw])
        cp = share(kw, l)
        if l == 0:
            build_dec(0, dec_chunks // 2)
        cp.wait_recv()
        halo_out[l] = mm(pick_h[...], msg[l]).astype(BF)
        arriving = []
        for j in range(4):
            peer = (g, lax.rem(d + offsets[j], n_dom), i)
            own = pl.ds(j * hb, hb)
            arriving.append(
                copy(halo_out.at[l, own, :], halo_in.at[l, own, :], h_send.at[l, j], h_recv.at[l, j], peer)
            )
            arriving[-1].start()
        halo_copies += arriving

        def local(r, l=l):
            esum[r, :] = mm(a_mesh[r, 0:md], msg[l])

        tiles(half, local)
        if l == 0:
            build_dec(dec_chunks // 2, dec_chunks)
            a_dec[...] = acc_dec[...].astype(BF)
            relay([6, 7, OUT])
        ready([kw + 1])
        for cp in arriving:
            cp.wait_recv()

        def update(r, l=l, kw=kw):
            total = (esum[r, :] + mm(a_mesh[r, md : md + 4 * hb], halo_in[l])).astype(BF)
            lat[r, :] = (lat[r, :].astype(F32) + silu(mm(total, weight(kw + 1)))).astype(BF)

        tiles(half, update)

    kd = n_w - 2
    ready([kd])
    cp = share(kd, layers)
    ready([n_w - 1, OUT])
    cp.wait_recv()
    dec_out[...] = mm(pick_d[...], msg[layers]).astype(BF)
    for j in range(4):
        peer = (g, lax.rem(d + offsets[j], n_dom), i)
        own = pl.ds(j * db, db)
        dec_copies.append(copy(dec_out.at[own, :], dec_in.at[own, :], d_send.at[j], d_recv.at[j], peer))
        dec_copies[-1].start()
    part = mm(a_dec[:, 0:md], msg[layers])
    for cp in dec_copies:
        cp.wait_recv()
    total = (part + mm(a_dec[:, md : md + 4 * db], dec_in[...])).astype(BF)
    mine = grid_lat[pl.ds(pl.multiple_of(i * quarter, quarter), quarter), :].astype(F32)
    new = (mine + silu(mm(total, weight(n_w - 1)))).astype(BF)
    head = jnp.concatenate([wo[q] for q in range(4)], axis=0)
    out[...] = mm(new, head)[:, 0:cin]

    for k in range(n_w + 2):
        to_sib(k).wait_send()
        to_x(k).wait_send()
        fwd(k).wait_send()
    for cp in base_copies + enc_copies + halo_copies + dec_copies + share_copies:
        cp.wait_send()


def per_device(n_dom, *args):
    grid_feat, mesh_base, w_msg = args[0], args[1], args[5]
    enc_row, halo_rows, dec_rows = args[13], args[17], args[21]
    gd, cin = grid_feat.shape
    md = mesh_base.shape[0]
    layers, width = w_msg.shape[0], w_msg.shape[1]
    half, quarter = md // 2, gd // 4
    n_enc, n_halo, n_dec = enc_row.shape[1], halo_rows.shape[1], dec_rows.shape[1]
    n_w = 4 + 2 * layers
    cin_pad = -(-cin // 128) * 128
    mesh_cols = md + -(-n_halo // 128) * 128
    dec_cols = md + -(-n_dec // 128) * 128
    V = pltpu.VMEM
    dma = pltpu.SemaphoreType.DMA
    scratch = [
        V((4, cin_pad, 128), BF),
        V((n_w, 4, width, 128), BF),
        V((4, 128, cin_pad), BF),
        V((4, half, 128), BF),
        V((gd, width), BF),
        V((gd, width), BF),
        V((half + n_enc, gd), BF),
        V((half + n_enc, gd), F32),
        V((half, mesh_cols), BF),
        V((half, mesh_cols), F32),
        V((quarter, dec_cols), BF),
        V((quarter, dec_cols), F32),
        V((n_halo, md), BF),
        V((n_dec, md), BF),
        V((n_enc, width), BF),
        V((n_enc, width), BF),
        V((half, width), F32),
        V((half, width), BF),
        V((layers + 1, md, width), BF),
        V((layers, n_halo, width), BF),
        V((layers, n_halo, width), BF),
        V((n_dec, width), BF),
        V((n_dec, width), BF),
        dma((n_w + 2,)), dma((n_w + 2,)), dma((n_w + 2,)), dma((n_w + 2,)), dma((n_w + 2,)), dma((n_w + 2,)),
        dma((3,)), dma((3,)),
        dma((4,)), dma((4,)), dma((layers, 4)), dma((layers, 4)), dma((4,)), dma((4,)),
        dma((layers + 1,)), dma((layers + 1,)),
    ]
    return pl.pallas_call(
        functools.partial(kernel, n_dom),
        out_shape=jax.ShapeDtypeStruct((quarter, cin), F32),
        in_specs=[pl.BlockSpec(memory_space=V)] * len(args),
        out_specs=pl.BlockSpec(memory_space=V),
        scratch_shapes=scratch,
        compiler_params=pltpu.CompilerParams(
            collective_id=0, has_side_effects=True, vmem_limit_bytes=56 * 1024 * 1024
        ),
    )(*args)


def solution(mesh):
    in_specs = (
        P(("groups", "dom"), None),
        P(("groups", "dom"), "mp"),
        P(None, "mp"),
        P(None, "mp"),
        P(None, "mp"),
        P(None, None, "mp"),
        P(None, None, "mp"),
        P(None, "mp"),
        P(None, "mp"),
        P("mp", None),
        P("dom", None),
        P("dom", None),
        P("dom", None),
        P("dom", None),
        P("dom", None),
        P("dom", None),
        P("dom", None),
        P(),
        P("dom", None),
        P("dom", None),
        P("dom", None),
        P(),
    )
    out_specs = P(("groups", "dom", "mp"), None)
    return jax.shard_map(
        functools.partial(per_device, mesh.shape["dom"]),
        mesh=mesh,
        in_specs=in_specs,
        out_specs=out_specs,
        check_vma=False,
    )
```

profile of v0, /device:TPU:0, one launch (start us, length us, event | category | flops | bytes accessed | tf_op | source)
XLA Modules:
  0.0 67.8 jit_solution(17173881405647897865)
XLA Ops:
  0.0 1.6 %copy.24.w_out = bf16[128,227]{1,0:T(8,128)(2,1)} copy(bf16[128,227]{0,1:T(8,128)(2,1)} %param.31) | data formatting | bytes 116224 | tf_op args[9]
  1.6 2.0 %copy.23.grid_feat = bf16[1024,227]{1,0:T(8,128)(2,1)} copy(bf16[1024,227]{0,1:T(8,128)(2,1)} %param.22) | data formatting | bytes 929792 | tf_op args[0]
  3.6 62.5 %shard_map.208 = f32[256,227]{1,0:T(8,128)} custom-call(bf16[1024,227]{1,0:T(8,128)(2,1)} %copy.23.grid_feat, bf16[1024,128]{1,0:T(8,128)(2,1)} %mesh_base.1, bf16[227,128]{1,0:T(8,128)(2,1)} %w_embed.1, bf16[512,128]{1,0:T(8,128)(2,1)} %w_edge.1, bf16[512,128]{1,0:T(8,128)(2,1)} %w_agg.1, bf16[2,512,128]{2,1,0:T(8,128)(2,1)} %w_msg.1, ...), custom_call_target="tpu_custom_call" | custom-call | tf_op jit(solution)/shard_map/pallas_call | solution.py:366
  66.1 1.8 %copy.25 = f32[256,227]{0,1:T(8,128)} copy(f32[256,227]{1,0:T(8,128)} %shard_map.208) | data formatting | bytes 464896 | tf_op jit(solution)/shard_map/pallas_call | solution.py:366
where the time goes:
time: 68.1 us; the launch traced here: 67.8 us
  Pallas kernels  62.5 us (92%)
  local copies, waits for them, and re-layouts  5.34 us (8%)
    pallas_call x1, Pallas kernels, per_device(): pl.pallas_call(functools.partial(kernel, n_dom), out_shape=jax.ShapeDtype...  62.5 us
    unnamed x2, local copies, waits for them, and re-layouts  3.57 us
    pallas_call x1, local copies, waits for them, and re-layouts, per_device(): pl.pallas_call(functools.partial(kernel, n_dom), out_shape=jax.ShapeDtype...  1.77 us

commit v1 on v0

--- a/solution.py
+++ b/solution.py
@@ -10,7 +10,7 @@
 MESH = pl.DeviceIdType.MESH
 BF = jnp.bfloat16
 F32 = jnp.float32
-CHUNK = 512
+CHUNK = 2048
 TILE = 256
 
 
@@ -21,6 +21,10 @@
 
 def mm(a, b):
     return jnp.dot(a, b, preferred_element_type=F32)
+
+
+def mm_tn(a, b):
+    return lax.dot_general(a, b, (((0,), (0,)), ((), ())), preferred_element_type=F32)
 
 
 def mm_nt(a, b):
@@ -38,12 +42,11 @@
     sib_send, sib_recv, x_send, x_recv, f_send, f_recv, b_send, b_recv,
     e_send, e_recv, h_send, h_recv, d_send, d_recv, g_send, g_recv,
 ):
-    gd = grid_feat.shape[0]
+    cin, gd = grid_feat.shape
     md = mesh_base.shape[0]
     half = md // 2
     quarter = gd // 4
     lat_w = wq.shape[2]
-    cin = grid_feat.shape[1]
     cap = enc_row.shape[1] // 4
     hb = halo_rows.shape[1] // 4
     db = dec_rows.shape[1] // 4
@@ -68,15 +71,12 @@
     emb_s[i] = jnp.zeros(emb_s.shape[1:], BF)
     emb_s[i, 0:cin, :] = w_embed[...]
     wo[i] = jnp.zeros(wo.shape[1:], BF)
-    wo[i, :, 0:cin] = w_out[...]
+    wo[i, 0:cin, :] = w_out[...]
     sources = [w_edge, w_agg]
     for l in range(layers):
         sources += [w_msg.at[l], w_upd.at[l]]
     sources += [w_dec, w_gup]
     n_w = len(sources)
-    for k in range(n_w):
-        wq[k, i] = sources[k][...]
-    base_s[i] = mesh_base[pl.ds(pl.multiple_of(c * half, half), half), :]
 
     EMB, OUT = n_w, n_w + 1
 
@@ -92,11 +92,14 @@
             src_ref=src, dst_ref=dst, send_sem=ss, recv_sem=rs, device_id=dev, device_id_type=MESH
         )
 
+    def own(k):
+        return sources[k] if k < n_w else slot(k, i)
+
     def to_sib(k):
-        return copy(slot(k, i), slot(k, i), sib_send.at[k], sib_recv.at[k], (g, d, sib))
+        return copy(own(k), slot(k, i), sib_send.at[k], sib_recv.at[k], (g, d, sib))
 
     def to_x(k):
-        return copy(slot(k, i), slot(k, i), x_send.at[k], x_recv.at[k], (g, d, xp))
+        return copy(own(k), slot(k, i), x_send.at[k], x_recv.at[k], (g, d, xp))
 
     def fwd(k):
         return copy(slot(k, xp), slot(k, xp), f_send.at[k], f_recv.at[k], (g, d, sib))
@@ -126,29 +129,43 @@
             to_sib(k).wait_recv()
             fwd(k).wait_recv()
 
-    launch([EMB, 0])
+    launch([EMB, 0, 1])
     for b in base_copies:
         b.start()
-    launch([1])
-
-    def build(src_ref, dst_ref, wt_ref, target_of, rows, cols, acc, lo, hi):
-        def body(t, _):
-            e = pl.ds(pl.multiple_of(t * CHUNK, CHUNK), CHUNK)
-            tgt = target_of(lax.broadcasted_iota(jnp.int32, (rows, CHUNK), 0))
-            dt = jnp.where(tgt == dst_ref[:, e], 1.0, 0.0).astype(BF)
-            row = lax.broadcasted_iota(jnp.int32, (cols, CHUNK), 0)
-            st = jnp.where(row == src_ref[:, e], wt_ref[:, e], 0.0).astype(BF)
-            acc[...] += mm_nt(dt, st)
-            return 0
-
-        lax.fori_loop(lo, hi, body, 0)
+    for k in range(n_w):
+        wq[k, i] = sources[k][...]
+    base_s[i] = mesh_base[my_rows, :]
+
+    def build(src_ref, dst_ref, wt_ref, target_of, source_of, rows, cols, size, t):
+        e = pl.ds(pl.multiple_of(t * size, size), size)
+        tgt = target_of(lax.broadcasted_iota(jnp.int32, (rows, size), 0))
+        dt = jnp.where(tgt == dst_ref[:, e], 1.0, 0.0).astype(BF)
+        src = source_of(lax.broadcasted_iota(jnp.int32, (cols, size), 0))
+        st = jnp.where(src == src_ref[:, e], wt_ref[:, e], 0.0).astype(BF)
+        return mm_nt(dt, st)
+
+    def mesh_order(m):
+        return jnp.where(m < half, m + c * half, jnp.where(m < md, m - c * half, m))
 
     def enc_target(m):
         return jnp.where(m < half, m + c * half, m + (md - half))
 
-    acc_enc[...] = jnp.zeros(acc_enc.shape, F32)
-    build(enc_src, enc_slot, enc_wt, enc_target, half + 4 * cap, gd, acc_enc, 0, enc_src.shape[1] // CHUNK)
-    a_enc[...] = acc_enc[...].astype(BF)
+    enc_size = min(CHUNK, enc_src.shape[1])
+    enc_steps = enc_src.shape[1] // enc_size
+
+    def build_enc(t):
+        return build(
+            enc_src, enc_slot, enc_wt, enc_target, lambda m: m, half + 4 * cap, gd, enc_size, t
+        )
+
+    if enc_steps == 1:
+        a_enc[...] = build_enc(0).astype(BF)
+    else:
+        acc_enc[...] = build_enc(0)
+        for t in range(1, enc_steps):
+            acc_enc[...] += build_enc(t)
+        a_enc[...] = acc_enc[...].astype(BF)
+    launch([2, 3])
 
     def weight(k):
         return jnp.concatenate([wq[k, q] for q in range(4)], axis=1)
@@ -162,11 +179,10 @@
 
     relay([EMB, 0])
     ready([EMB])
-    launch([2, 3])
 
     def embed(r):
         w = jnp.concatenate([emb_s[q] for q in range(4)], axis=1)[0:cin]
-        grid_lat[r, :] = silu(mm(grid_feat[r, :], w)).astype(BF)
+        grid_lat[r, :] = silu(mm_tn(grid_feat[:, r], w)).astype(BF)
 
     tiles(gd, embed)
     ready([0])
@@ -177,19 +193,26 @@
     tiles(gd, edge)
 
     slots = pl.ds(half, 4 * cap)
-    enc_out[...] = mm(a_enc[slots, :], sent[...]).astype(BF)
-    enc_copies, halo_copies, dec_copies = [], [], []
-    for j in range(4):
-        peer = (g, lax.rem(d + offsets[j], n_dom), i)
-        own = pl.ds(j * cap, cap)
-        enc_copies.append(copy(enc_out.at[own, :], enc_in.at[own, :], e_send.at[j], e_recv.at[j], peer))
-        enc_copies[-1].start()
+    def exchange(value, out_ref, in_ref, rows, send, recv):
+        out_ref[...] = value.astype(BF)
+        copies = []
+        for j in range(4):
+            peer = (g, lax.rem(d + offsets[j], n_dom), i)
+            part = pl.ds(j * rows, rows)
+            copies.append(copy(out_ref.at[part, :], in_ref.at[part, :], send.at[j], recv.at[j], peer))
+            copies[-1].start()
+        return copies
+
+    enc_copies = exchange(mm(a_enc[slots, :], sent[...]), enc_out, enc_in, cap, e_send, e_recv)
+    halo_copies = []
 
     def enc_local(r):
         esum[r, :] = mm(a_enc[r, :], sent[...])
 
     tiles(half, enc_local)
     relay([1])
+
+    launch([4, 5])
 
     def pick(rows_ref, ref):
         n = ref.shape[0]
@@ -197,15 +220,16 @@
         col = jnp.broadcast_to(row, (128, n)).T
         lane = lax.broadcasted_iota(jnp.int32, (n, 128), 1).astype(F32)
         for b in range(md // 128):
-            ref[:, b * 128 : (b + 1) * 128] = jnp.where(col == lane + 128.0 * b, 1.0, 0.0).astype(BF)
+            shift = c * half if b * 128 < half else -c * half
+            here = lane + (128 * b + shift).astype(F32)
+            ref[:, b * 128 : (b + 1) * 128] = jnp.where(col == here, 1.0, 0.0).astype(BF)
 
     pick(halo_rows, pick_h)
     pick(dec_rows, pick_d)
 
-    acc_mesh[...] = jnp.zeros(acc_mesh.shape, F32)
-    acc_dec[...] = jnp.zeros(acc_dec.shape, F32)
-    mesh_chunks = mesh_src.shape[1] // CHUNK
-    dec_chunks = dec_src.shape[1] // CHUNK
+    mesh_size = CHUNK
+    mesh_chunks = mesh_src.shape[1] // mesh_size
+    dec_size = dec_src.shape[1] // 2
     mesh_cols = acc_mesh.shape[1]
 
     def mesh_target(m):
@@ -214,19 +238,25 @@
     def dec_target(m):
         return m + i * quarter
 
-    def build_mesh(lo, hi):
-        build(mesh_src, mesh_dst, mesh_wt, mesh_target, half, mesh_cols, acc_mesh, lo, hi)
-
-    def build_dec(lo, hi):
-        build(dec_src, dec_dst, dec_wt, dec_target, quarter, acc_dec.shape[1], acc_dec, lo, hi)
-
-    build_mesh(0, mesh_chunks // 2)
+    def build_mesh(t):
+        return build(
+            mesh_src, mesh_dst, mesh_wt, mesh_target, mesh_order, half, mesh_cols, mesh_size, t
+        )
+
+    def build_dec(t):
+        return build(
+            dec_src, dec_dst, dec_wt, dec_target, mesh_order, quarter, acc_dec.shape[1], dec_size, t
+        )
+
+    def mesh_step(t, _):
+        acc_mesh[...] += build_mesh(t)
+        return 0
+
+    acc_mesh[...] = build_mesh(0)
     relay([2, 3])
-    launch([4, 5])
-    build_mesh(mesh_chunks // 2, mesh_chunks)
-    a_mesh[...] = acc_mesh[...].astype(BF)
+    launch([6, 7, OUT])
+    lax.fori_loop(1, mesh_chunks - 1, mesh_step, 0)
     relay([4, 5])
-    launch([6, 7, OUT])
 
     for cp in enc_copies:
         cp.wait_recv()
@@ -247,40 +277,46 @@
 
     def share(k, t):
         def body(r):
-            there = pl.ds(pl.multiple_of(c * half + r.start, TILE), TILE)
-            msg[t, there, :] = silu(mm(lat[r, :], weight(k))).astype(BF)
+            msg[t, r, :] = silu(mm(lat[r, :], weight(k))).astype(BF)
 
         tiles(half, body)
-        cp = copy(msg.at[t, my_rows, :], msg.at[t, my_rows, :], g_send.at[t], g_recv.at[t], (g, d, sib))
+        cp = copy(
+            msg.at[t, pl.ds(0, half), :], msg.at[t, pl.ds(half, half), :],
+            g_send.at[t], g_recv.at[t], (g, d, sib),
+        )
         cp.start()
         share_copies.append(cp)
         return cp
 
+    near, far = pl.ds(0, half), pl.ds(half, half)
     for l in range(layers):
         kw = 2 + 2 * l
         ready([kw])
         cp = share(kw, l)
+        picked = mm(pick_h[:, 0:half], msg[l, near, :])
         if l == 0:
-            build_dec(0, dec_chunks // 2)
+            a_mesh[...] = (acc_mesh[...] + build_mesh(mesh_chunks - 1)).astype(BF)
+        else:
+            acc_dec[...] += build_dec(1)
+            a_dec[...] = acc_dec[...].astype(BF)
+
+        def local(r, l=l):
+            esum[r, :] = mm(a_mesh[r, 0:half], msg[l, near, :])
+
+        tiles(half, local)
         cp.wait_recv()
-        halo_out[l] = mm(pick_h[...], msg[l]).astype(BF)
-        arriving = []
-        for j in range(4):
-            peer = (g, lax.rem(d + offsets[j], n_dom), i)
-            own = pl.ds(j * hb, hb)
-            arriving.append(
-                copy(halo_out.at[l, own, :], halo_in.at[l, own, :], h_send.at[l, j], h_recv.at[l, j], peer)
-            )
-            arriving[-1].start()
+        arriving = exchange(
+            picked + mm(pick_h[:, half:md], msg[l, far, :]),
+            halo_out.at[l], halo_in.at[l], hb, h_send.at[l], h_recv.at[l],
+        )
         halo_copies += arriving
 
         def local(r, l=l):
-            esum[r, :] = mm(a_mesh[r, 0:md], msg[l])
+            esum[r, :] += mm(a_mesh[r, half:md], msg[l, far, :])
 
         tiles(half, local)
         if l == 0:
-            build_dec(dec_chunks // 2, dec_chunks)
-            a_dec[...] = acc_dec[...].astype(BF)
+            acc_dec[...] = build_dec(0)
             relay([6, 7, OUT])
         ready([kw + 1])
         for cp in arriving:
@@ -295,22 +331,21 @@
     kd = n_w - 2
     ready([kd])
     cp = share(kd, layers)
+    picked = mm(pick_d[:, 0:half], msg[layers, near, :])
+    part = mm(a_dec[:, 0:half], msg[layers, near, :])
     ready([n_w - 1, OUT])
     cp.wait_recv()
-    dec_out[...] = mm(pick_d[...], msg[layers]).astype(BF)
-    for j in range(4):
-        peer = (g, lax.rem(d + offsets[j], n_dom), i)
-        own = pl.ds(j * db, db)
-        dec_copies.append(copy(dec_out.at[own, :], dec_in.at[own, :], d_send.at[j], d_recv.at[j], peer))
-        dec_copies[-1].start()
-    part = mm(a_dec[:, 0:md], msg[layers])
+    dec_copies = exchange(
+        picked + mm(pick_d[:, half:md], msg[layers, far, :]), dec_out, dec_in, db, d_send, d_recv
+    )
+    part = part + mm(a_dec[:, half:md], msg[layers, far, :])
     for cp in dec_copies:
         cp.wait_recv()
     total = (part + mm(a_dec[:, md : md + 4 * db], dec_in[...])).astype(BF)
     mine = grid_lat[pl.ds(pl.multiple_of(i * quarter, quarter), quarter), :].astype(F32)
     new = (mine + silu(mm(total, weight(n_w - 1)))).astype(BF)
-    head = jnp.concatenate([wo[q] for q in range(4)], axis=0)
-    out[...] = mm(new, head)[:, 0:cin]
+    head = jnp.concatenate([wo[q] for q in range(4)], axis=1)
+    out[...] = mm_nt(head, new)[0:cin, :]
 
     for k in range(n_w + 2):
         to_sib(k).wait_send()
@@ -321,9 +356,10 @@
 
 
 def per_device(n_dom, *args):
+    args = (args[0].T,) + args[1:9] + (args[9].T,) + args[10:]
     grid_feat, mesh_base, w_msg = args[0], args[1], args[5]
     enc_row, halo_rows, dec_rows = args[13], args[17], args[21]
-    gd, cin = grid_feat.shape
+    cin, gd = grid_feat.shape
     md = mesh_base.shape[0]
     layers, width = w_msg.shape[0], w_msg.shape[1]
     half, quarter = md // 2, gd // 4
@@ -337,7 +373,7 @@
     scratch = [
         V((4, cin_pad, 128), BF),
         V((n_w, 4, width, 128), BF),
-        V((4, 128, cin_pad), BF),
+        V((4, cin_pad, 128), BF),
         V((4, half, 128), BF),
         V((gd, width), BF),
         V((gd, width), BF),
@@ -365,14 +401,14 @@
     ]
     return pl.pallas_call(
         functools.partial(kernel, n_dom),
-        out_shape=jax.ShapeDtypeStruct((quarter, cin), F32),
+        out_shape=jax.ShapeDtypeStruct((cin, quarter), F32),
         in_specs=[pl.BlockSpec(memory_space=V)] * len(args),
         out_specs=pl.BlockSpec(memory_space=V),
         scratch_shapes=scratch,
         compiler_params=pltpu.CompilerParams(
             collective_id=0, has_side_effects=True, vmem_limit_bytes=56 * 1024 * 1024
         ),
-    )(*args)
+    )(*args).T
 
 
 def solution(mesh):

time: 68.1 us -> 61.9 us (0.909)
  local copies, waits for them, and re-layouts: 5.34 us -> 1.65 us
  Pallas kernels: 62.5 us -> 59.7 us
    pallas_call x1, Pallas kernels: 62.5 us -> 59.7 us  [per_device(): pl.pallas_call(functools.partial(kernel, n_dom), out_shape=jax.ShapeDtype...]
    unnamed x2 -> x1, local copies, waits for them, and re-layouts: 3.57 us -> 1.65 us
    pallas_call x1 -> x0, local copies, waits for them, and re-layouts: 1.77 us -> none  [per_device(): pl.pallas_call(functools.partial(kernel, n_dom), out_shape=jax.ShapeDtype...]
where the time goes in v1:
time: 61.9 us; the launch traced here: 61.3 us
  Pallas kernels  59.7 us (96%)
  local copies, waits for them, and re-layouts  1.65 us (3%)
    pallas_call x1, Pallas kernels, per_device(): pl.pallas_call(functools.partial(kernel, n_dom), out_shape=jax.ShapeDtype...  59.7 us
    unnamed x1, local copies, waits for them, and re-layouts  1.65 us

profile of v1, /device:TPU:0, one launch (start us, length us, event | category | flops | bytes accessed | tf_op | source)
XLA Modules:
  0.0 61.3 jit_solution(5255783987333373602)
XLA Ops:
  0.0 59.7 %shard_map.208 = f32[227,256]{1,0:T(8,128)} custom-call(bf16[227,1024]{1,0:T(8,128)(2,1)} %bitcast.4, bf16[1024,128]{1,0:T(8,128)(2,1)} %mesh_base.1, bf16[227,128]{1,0:T(8,128)(2,1)} %w_embed.1, bf16[512,128]{1,0:T(8,128)(2,1)} %w_edge.1, bf16[512,128]{1,0:T(8,128)(2,1)} %w_agg.1, bf16[2,512,128]{2,1,0:T(8,128)(2,1)} %w_msg.1, bf16[2,512,128]{2,1,0:T(8,128)(2,1)} %w_upd.1, ...), custom_call_target="tpu_custom_call" | custom-call | tf_op jit(solution)/shard_map/pallas_call | solution.py:402
  59.7 1.6 %copy.24 = f32[256,227]{0,1:T(8,128)} copy(f32[256,227]{0,1:T(8,128)} %bitcast.3) | data formatting | bytes 464896
